TPU v7x, 32 devices: a whole 2x2x4 slice. The times are simulated.
32 devices in a mesh: groups: 2 (over x), goal: 16 (over z, y, core).
Axes of the slice: x: 2, y: 2, z: 4, core: 2. Of those that a mesh axis runs over, the one named last changes fastest.
Arguments:
- queries: bfloat16 [128, 64, 4096], P(('groups', 'goal')), parts along dimension 0, may hold values from -8 to 8
- goal_keys: bfloat16 [32, 256, 4096], P(('groups', 'goal')), parts along dimension 0, may hold values from -8 to 8
- goal_values: bfloat16 [32, 256, 4096], P(('groups', 'goal')), parts along dimension 0, may hold values from -6 to 6
- out_weight: bfloat16 [4096, 2048], P('goal'), may hold values from -0.5 to 0.5
- tactic_goal: int32 [128, 1], P(('groups', 'goal')), parts along dimension 0, may hold values from 0 to 15
- tactic_len: int32 [128], P(('groups', 'goal')), parts along dimension 0, may hold values from 1 to 64
Outputs:
- projected: bfloat16 [128, 64, 2048], P(('groups', 'goal')), parts along dimension 0
There are 2 independent parts, one for each index of `groups`. A program takes and returns all parts, laid end to end along the dimension named above; an argument that names none is the same for every part. Nothing has to cross between parts.
Inputs may be any that keep to these rules, and one draw needn't show every extreme that they name: `tactic_goal`: every goal is read by at least one tactic; tactics per goal are uneven. `tactic_len`: the live positions of a tactic are its leading ones.
All inputs are finite; a program needn't handle non-finite values.
Results may differ from a plain program's by a relative error of at most 0.01.
Values may be sent and summed in bfloat16 or wider, within the bound.
A program may use at most 192 MiB of HBM per device.

v0:
```python
import math

import jax
import jax.numpy as jnp
from jax import lax
from jax.sharding import PartitionSpec as P

DH = 64


def attend_block(query_block, keys_heads, values_heads, block_ids):
    tact_count = query_block.shape[0]
    row_count = query_block.shape[1]
    width_local = query_block.shape[2]
    head_count = width_local // DH
    keys_tact = jnp.take(keys_heads, block_ids, axis=0).reshape(tact_count, -1, head_count, DH)
    vals_tact = jnp.take(values_heads, block_ids, axis=0).reshape(tact_count, -1, head_count, DH)
    query_four = query_block.reshape(tact_count, row_count, head_count, DH)
    scores = jnp.einsum(
        "tihd,tjhd->thij", query_four, keys_tact, preferred_element_type=jnp.float32
    )
    biggest = jnp.max(scores, axis=-1, keepdims=True)
    powers = jnp.exp(scores - biggest)
    weights = (powers / jnp.sum(powers, axis=-1, keepdims=True)).astype(jnp.bfloat16)
    attended = jnp.einsum("thij,tjhd->tihd", weights, vals_tact, preferred_element_type=jnp.float32)
    return attended.reshape(tact_count, row_count, width_local).astype(jnp.bfloat16)


def attend(query_piece, keys_heads, values_heads, goal_ids):
    tact_count = query_piece.shape[0]
    row_count = query_piece.shape[1]
    width_local = query_piece.shape[2]
    block_size = math.gcd(tact_count, 64)
    block_count = tact_count // block_size
    query_blocks = query_piece.reshape(block_count, block_size, row_count, width_local)
    id_blocks = goal_ids.reshape(block_count, block_size)

    def one_block(operands):
        return attend_block(operands[0], keys_heads, values_heads, operands[1])

    results = lax.map(one_block, (query_blocks, id_blocks))
    return results.reshape(tact_count, row_count, width_local)


def shards(queries, goal_keys, goal_values, out_weight, tactic_goal, tactic_len):
    goal_ids = lax.all_gather(tactic_goal[:, 0], "goal", axis=0, tiled=True)
    keys_heads, values_heads = (
        lax.all_to_all(goal_keys, "goal", split_axis=2, concat_axis=0, tiled=True),
        lax.all_to_all(goal_values, "goal", split_axis=2, concat_axis=0, tiled=True),
    )
    query_heads = lax.all_to_all(queries, "goal", split_axis=2, concat_axis=0, tiled=True)
    attended = attend(query_heads, keys_heads, values_heads, goal_ids)
    merged = lax.all_to_all(attended, "goal", split_axis=0, concat_axis=2, tiled=True)
    live_rows = jnp.arange(merged.shape[1])[None, :] < tactic_len[:, None]
    context = jnp.where(live_rows[:, :, None], merged, jnp.zeros_like(merged))
    tact_local = context.shape[0]
    row_count = context.shape[1]
    flat = context.reshape(tact_local * row_count, context.shape[2])
    projected = jnp.dot(
        flat,
        lax.all_gather(out_weight, "goal", axis=0, tiled=True),
        preferred_element_type=jnp.float32,
    )
    return projected.astype(jnp.bfloat16).reshape(tact_local, row_count, out_weight.shape[1])


def solution(mesh):
    return jax.shard_map(
        shards,
        mesh=mesh,
        in_specs=(
            P(("groups", "goal"), None, None),
            P(("groups", "goal"), None, None),
            P(("groups", "goal"), None, None),
            P("goal", None),
            P(("groups", "goal"), None),
            P(("groups", "goal")),
        ),
        out_specs=P(("groups", "goal"), None, None),
        check_vma=False,
    )
```

profile of v0, /device:TPU:13, one launch (start us, length us, event | category | flops | bytes accessed | tf_op | source)
XLA Modules:
  0.0 509.1 jit_solution(2314349538631211243)
XLA Ops:
  6.5 0.0 all-gather.3.cloned.1.call-start
  6.5 0.7 all-gather.3.cloned.1.call-update
  7.3 10.1 %copy.23 = bf16[1,256,4096]{1,0,2:T(2,128)(2,1)} copy(bf16[1,256,4096]{2,1,0:T(8,128)(2,1)} %param.10) | data formatting | bytes 4194304 | tf_op args[2]
  17.3 0.5 broadcast.32
  17.8 21.7 %reduce.1 = bf16[4096,256]{1,0:T(8,128)(2,1)S(1)} reduce(bf16[4096,1,256]{2,1,0:T(2,128)(2,1)} %bitcast.58, bf16[]{:T(256)} %broadcast.32), dimensions={1}, to_apply=%bitcast.44.reduce_sub_computation | reduce | bytes 4194306
  39.5 2.1 reshape.91
  41.6 6.6 %all-to-all-start = ((bf16[16,2,32768]{2,1,0:T(2,128)(2,1)}), bf16[16,2,32768]{2,1,0:T(2,128)(2,1)S(1)}, u32[]{:S(2)}, u32[]{:S(2)}) async-start(bf16[16,2,32768]{2,1,0:T(2,128)(2,1)} %reshape.91), calls=%async_computation | async-start | bytes 4194304 | tf_op jit(solution)/shard_map/all_to_all | solution.py:49
  48.1 10.1 %copy.26 = bf16[1,256,4096]{1,0,2:T(2,128)(2,1)} copy(bf16[1,256,4096]{2,1,0:T(8,128)(2,1)} %param.9) | data formatting | bytes 4194304 | tf_op args[1]
  58.2 23.0 %reduce = bf16[4096,256]{1,0:T(8,128)(2,1)} reduce(bf16[4096,1,256]{2,1,0:T(2,128)(2,1)} %bitcast.59, bf16[]{:T(256)} %broadcast.32), dimensions={1}, to_apply=%bitcast.46.reduce_sub_computation | reduce | bytes 4194306
  81.1 4.0 reshape.93
  85.1 58.2 %all-to-all-done = bf16[16,2,32768]{2,1,0:T(2,128)(2,1)S(1)} async-done(((bf16[16,2,32768]{2,1,0:T(2,128)(2,1)}), bf16[16,2,32768]{2,1,0:T(2,128)(2,1)S(1)}, u32[]{:S(2)}, u32[]{:S(2)}) %all-to-all-start) | async-done | bytes 2097184 | tf_op jit(solution)/shard_map/all_to_all | solution.py:49
  143.3 4.3 all-to-all-start.1
  147.7 0.0 copy-start.2
  147.7 0.0 copy-start
  147.7 7.0 %copy.29 = bf16[4,64,4096]{1,0,2:T(4,128)(2,1)} copy(bf16[4,64,4096]{2,1,0:T(8,128)(2,1)} %param.8) | data formatting | bytes 4194304 | tf_op args[0]
  154.7 7.5 %reshape.95 = bf16[16,2,32768]{2,1,0:T(2,128)(2,1)} reshape(bf16[4096,4,64]{2,1,0:T(4,128)(2,1)} %bitcast.63) | data formatting | bytes 4194304
  162.3 52.0 %all-to-all-done.1 = bf16[16,2,32768]{2,1,0:T(2,128)(2,1)} async-done(((bf16[16,2,32768]{2,1,0:T(2,128)(2,1)}), bf16[16,2,32768]{2,1,0:T(2,128)(2,1)}, u32[]{:S(2)}, u32[]{:S(2)}) %all-to-all-start.1) | async-done | bytes 2097184 | tf_op jit(solution)/shard_map/all_to_all | solution.py:48
  214.3 4.7 all-to-all-start.2
  219.0 0.0 copy-done.2
  219.0 0.6 dynamic-slice.1
  220.3 0.0 copy-done
  220.3 0.1 bitcast_dynamic-update-slice_fusion
  220.4 44.1 %all-reduce = s32[64]{0:T(128)S(1)} all-reduce(s32[64]{0:T(128)S(1)} %bitcast_dynamic-update-slice_fusion), channel_id=2, replica_groups=mesh['groups'=2,'goal'=16] {'goal'}, use_global_device_ids=true, to_apply=%add | all-reduce | flops 64 | bytes 512 | tf_op jit(solution)/shard_map/all_gather | solution.py:46
  264.5 6.8 %reshape.92 = bf16[4096,1,256]{2,1,0:T(2,128)(2,1)} reshape(bf16[16,2,32768]{2,1,0:T(2,128)(2,1)S(1)} %all-to-all-done) | data formatting | bytes 4194304
  271.3 3.9 copy.34
  275.1 2.8 copy.24
  278.0 10.5 %reshape.94 = bf16[4096,1,256]{2,1,0:T(2,128)(2,1)} reshape(bf16[16,2,32768]{2,1,0:T(2,128)(2,1)} %all-to-all-done.1) | data formatting | bytes 4194304
  288.5 3.9 copy.35
  292.4 3.9 copy.27
  296.3 5.5 %gather_fusion = bf16[64,256,256]{2,1,0:T(8,128)(2,1)} fusion(bf16[16,256,256]{2,1,0:T(8,128)(2,1)S(1)} %bitcast.56, s32[1024]{0:T(1024)S(1)} %pad_clamp_fusion), kind=kCustom, calls=%fused_computation.clone | custom fusion | bytes 16777472 | tf_op jit(solution)/shard_map/while/body/eval_jaxpr/jit(_take)/gather | solution.py:17
  301.8 7.1 %gather_fusion.1 = bf16[64,256,256]{2,1,0:T(8,128)(2,1)} fusion(bf16[16,256,256]{2,1,0:T(8,128)(2,1)} %bitcast.57, s32[1024]{0:T(1024)S(1)} %pad_clamp_fusion), kind=kCustom, calls=%fused_computation.1.clone | custom fusion | bytes 16777472 | tf_op jit(solution)/shard_map/while/body/eval_jaxpr/jit(_take)/gather | solution.py:16
  308.9 11.6 %broadcast_select_fusion = (bf16[64,256,256]{2,1,0:T(8,128)(2,1)}, bf16[64,256,256]{2,1,0:T(8,128)(2,1)}) fusion(bf16[64,256,256]{2,1,0:T(8,128)(2,1)} %gather_fusion.1, pred[64]{0:T(512)(128)(4,1)S(1)} %compare_and_fusion, bf16[64,256,256]{2,1,0:T(8,128)(2,1)} %gather_fusion), kind=kLoop, calls=%fused_computation.9 | loop fusion | flops 8388608 | bytes 33554496 | tf_op jit(solution)/shard_map/while/body/eval_jaxpr/jit(_take)/select_n | solution.py:16
  320.5 11.9 %copy.28 = bf16[64,256,256]{1,2,0:T(8,128)(2,1)} copy(bf16[64,256,256]{2,1,0:T(8,128)(2,1)} %get-tuple-element.16) | data formatting | bytes 16777216 | tf_op jit(solution)/shard_map/while/body/eval_jaxpr/jit(_take)/select_n | solution.py:16
  332.4 0.0 all-to-all-done.2
  332.4 7.5 %reshape.96 = bf16[4096,4,64]{2,1,0:T(4,128)(2,1)} reshape(bf16[16,2,32768]{2,1,0:T(2,128)(2,1)} %all-to-all-done.2) | data formatting | bytes 4194304
  339.9 5.4 %copy.30 = bf16[4,64,16,256]{3,1,0,2:T(8,128)(2,1)S(1)} copy(bf16[4,64,16,256]{1,0,3,2:T(4,128)(2,1)} %bitcast.62) | data formatting | bytes 4194304 | tf_op jit(solution)/shard_map/all_to_all | solution.py:51
  345.2 3.3 reshape.60
  348.5 11.9 %copy.25 = bf16[64,256,256]{1,2,0:T(8,128)(2,1)} copy(bf16[64,256,256]{2,1,0:T(8,128)(2,1)} %get-tuple-element.17) | data formatting | bytes 16777216 | tf_op jit(solution)/shard_map/while/body/eval_jaxpr/jit(_take)/select_n | solution.py:17
  360.4 12.7 %fusion.6 = f32[64,4,256,64]{2,3,1,0:T(8,128)} fusion(bf16[64,256,4,64]{1,3,2,0:T(8,128)(2,1)} %bitcast.55, bf16[64,64,4,64]{3,2,1,0:T(4,128)(2,1)} %reshape.60), kind=kOutput, calls=%fused_computation.11 | convolution fusion | flops 536870912 | bytes 27262976 | tf_op jit(solution)/shard_map/while/body/eval_jaxpr/tihd,tjhd->thij/dot_general | solution.py:19
  373.1 14.6 %fusion.18 = f32[64,4,64]{2,1,0:T(4,128)S(1)} fusion(f32[64,4,256,64]{2,3,1,0:T(8,128)} %fusion.6), kind=kOutput, calls=%fused_computation.25 | output fusion | flops 8388863 | bytes 16842752 | tf_op jit(solution)/shard_map/while/body/eval_jaxpr/sub | solution.py:23
  387.7 43.3 %fusion.8 = bf16[64,4,64,64]{3,2,1,0:T(8,128)(2,1)} fusion(bf16[64,256,4,64]{1,3,2,0:T(8,128)(2,1)} %bitcast.67, f32[64,4,64]{2,1,0:T(4,128)S(1)} %fusion.18, f32[64,4,256,64]{2,3,1,0:T(8,128)} %fusion.6), kind=kOutput, calls=%fused_computation.13 | convolution fusion | flops 550519040 | bytes 27328512 | tf_op jit(solution)/shard_map/while/body/eval_jaxpr/thij,tjhd->tihd/dot_general | solution.py:25
  431.0 0.0 copy-start.1
  431.0 4.8 copy.32
  435.8 7.5 %all-to-all-start.3 = ((bf16[64,64,256]{2,1,0:T(8,128)(2,1)}), bf16[64,64,256]{2,1,0:T(8,128)(2,1)S(1)}, u32[]{:S(2)}, u32[]{:S(2)}) async-start(bf16[64,64,256]{2,1,0:T(8,128)(2,1)} %copy.32), calls=%async_computation.3 | async-start | bytes 4194304 | tf_op jit(solution)/shard_map/all_to_all | solution.py:53
  443.4 0.0 copy-done.1
  443.4 0.1 iota_compare_fusion
  443.4 0.1 lt.30
  443.5 47.3 %all-to-all-done.3 = bf16[64,64,256]{2,1,0:T(8,128)(2,1)S(1)} async-done(((bf16[64,64,256]{2,1,0:T(8,128)(2,1)}), bf16[64,64,256]{2,1,0:T(8,128)(2,1)S(1)}, u32[]{:S(2)}, u32[]{:S(2)}) %all-to-all-start.3) | async-done | bytes 2097184 | tf_op jit(solution)/shard_map/all_to_all | solution.py:53
  490.8 1.2 copy.33
  492.0 0.9 copy.36
  492.9 0.0 all-gather.3.cloned.1.call-done
  492.9 9.3 %convolution_convert_fusion = bf16[256,2048]{1,0:T(8,128)(2,1)} fusion(bf16[4096,2048]{1,0:T(8,128)(2,1)} %all-gather.3.cloned.1.call-done, bf16[256,4096]{1,0:T(8,128)(2,1)S(1)} %bitcast.71, pred[256]{0:T(512)(128)(4,1)S(1)} %lt.30), kind=kOutput, calls=%fused_computation.14 | convolution fusion | flops 4296540160 | bytes 19923200 | tf_op jit(solution)/shard_map/dot_general | solution.py:59
  (4 shorter events, 0.0 us)
Async XLA Ops:
  6.5 486.4 %all-gather.3.cloned.1.call-start = ((), (), s32[]{:S(2)}) async-start(), calls=%async_computation.4 | async-start | bytes 17825792 | tf_op jit(solution)/shard_map/all_gather | solution.py:61
  41.6 101.8 %all-to-all-start = ((bf16[16,2,32768]{2,1,0:T(2,128)(2,1)}), bf16[16,2,32768]{2,1,0:T(2,128)(2,1)S(1)}, u32[]{:S(2)}, u32[]{:S(2)}) async-start(bf16[16,2,32768]{2,1,0:T(2,128)(2,1)} %reshape.91), calls=%async_computation | async-start | bytes 4194304 | tf_op jit(solution)/shard_map/all_to_all | solution.py:49
  143.3 71.0 %all-to-all-start.1 = ((bf16[16,2,32768]{2,1,0:T(2,128)(2,1)}), bf16[16,2,32768]{2,1,0:T(2,128)(2,1)}, u32[]{:S(2)}, u32[]{:S(2)}) async-start(bf16[16,2,32768]{2,1,0:T(2,128)(2,1)} %reshape.93), calls=%async_computation.1 | async-start | bytes 4194304 | tf_op jit(solution)/shard_map/all_to_all | solution.py:48
  147.7 71.4 %copy-start.2 = (u32[32]{0:T(128)S(1)}, u32[32]{0:T(128)}, u32[]{:S(2)}) copy-start(u32[32]{0:T(128)} %constant.37) | copy-start | bytes 388
  147.7 72.6 %copy-start = (s32[4,1]{0,1:T(1,128)S(1)}, s32[4,1]{0,1:T(1,128)}, u32[]{:S(2)}) copy-start(s32[4,1]{0,1:T(1,128)} %param.12) | copy-start | bytes 52
  214.3 118.1 %all-to-all-start.2 = ((bf16[16,2,32768]{2,1,0:T(2,128)(2,1)}), bf16[16,2,32768]{2,1,0:T(2,128)(2,1)}, u32[]{:S(2)}, u32[]{:S(2)}) async-start(bf16[16,2,32768]{2,1,0:T(2,128)(2,1)} %reshape.95), calls=%async_computation.2 | async-start | bytes 4194304 | tf_op jit(solution)/shard_map/all_to_all | solution.py:51
  431.0 12.3 %copy-start.1 = (s32[4]{0:T(128)S(1)}, s32[4]{0:T(128)}, u32[]{:S(2)}) copy-start(s32[4]{0:T(128)} %param.13) | copy-start | bytes 52
  435.8 54.9 %all-to-all-start.3 = ((bf16[64,64,256]{2,1,0:T(8,128)(2,1)}), bf16[64,64,256]{2,1,0:T(8,128)(2,1)S(1)}, u32[]{:S(2)}, u32[]{:S(2)}) async-start(bf16[64,64,256]{2,1,0:T(8,128)(2,1)} %copy.32), calls=%async_computation.3 | async-start | bytes 4194304 | tf_op jit(solution)/shard_map/all_to_all | solution.py:53
Sparse Core Ops, SparseCore 0:
  9.5 193.1 all-gather.2
where the time goes:
time: 512 us; the launch traced here: 509 us
  waiting for transfers between devices  158 us (31%)
  local copies, waits for them, and re-layouts  133 us (26%)
  other arithmetic  70.9 us (14%)
  matrix products  65.3 us (13%)
  blocking collectives  44.1 us (9%)
  starting transfers between devices  23.2 us (5%)
  between operations  14.2 us (3%)
    unnamed x22, local copies, waits for them, and re-layouts  75.4 us
    all_to_all x1, waiting for transfers between devices, shards(): lax.all_to_all(goal_values, 'goal', split_axis=2, concat_axis=0, tiled=True)  58.2 us
    all_to_all x1, waiting for transfers between devices, shards(): lax.all_to_all(goal_keys, 'goal', split_axis=2, concat_axis=0, tiled=True)  52 us
    all_to_all x1, waiting for transfers between devices, shards(): lax.all_to_all(attended, 'goal', split_axis=0, concat_axis=2, tiled=True)  47.3 us
    unnamed x2, other arithmetic  44.6 us
    all_gather x1, blocking collectives, shards(): goal_ids = lax.all_gather(tactic_goal[:, 0], 'goal', axis=0, tiled=True)  44.1 us
    dot_general x1, matrix products, attend_block(): jnp.einsum('thij,tjhd->tihd', weights, vals_tact, preferred_element_type=...  43.3 us
    sub x1, other arithmetic, attend_block(): powers = jnp.exp(scores - biggest)  14.6 us
  transfers between devices with their start and end apart: 5, of which 3 were waited for; matrix products, arithmetic and copies ran while one was open for 51% of the time, Pallas kernels for 0%

commit v1 on v0

v1 whole, which is shorter than its diff:
```python
import functools

import jax
import jax.numpy as jnp
from jax import lax
from jax.experimental import pallas as pl
from jax.experimental.pallas import tpu as pltpu
from jax.sharding import PartitionSpec as P

DH = 64
LANES = 128
MESH = pl.DeviceIdType.MESH


def attend(query_piece, keys_heads, values_heads, goal_ids):
    row_count = query_piece.shape[1]
    width_local = query_piece.shape[2]
    head_count = width_local // DH

    def one_tactic(operands):
        query_rows, goal = operands
        keys = lax.dynamic_index_in_dim(keys_heads, goal, 0, keepdims=False).reshape(-1, head_count, DH)
        values = lax.dynamic_index_in_dim(values_heads, goal, 0, keepdims=False).reshape(-1, head_count, DH)
        query_three = query_rows.reshape(row_count, head_count, DH)
        scores = jnp.einsum("ihd,jhd->hij", query_three, keys, preferred_element_type=jnp.float32)
        powers = jnp.exp(scores - jnp.max(scores, axis=-1, keepdims=True))
        weights = (powers / jnp.sum(powers, axis=-1, keepdims=True)).astype(jnp.bfloat16)
        attended = jnp.einsum("hij,jhd->ihd", weights, values, preferred_element_type=jnp.float32)
        return attended.reshape(row_count, width_local).astype(jnp.bfloat16)

    return lax.map(one_tactic, (query_piece, goal_ids))


def plain_shards(queries, goal_keys, goal_values, out_weight, tactic_goal, tactic_len):
    goal_ids = lax.all_gather(tactic_goal[:, 0], "goal", axis=0, tiled=True)
    keys_heads, values_heads = (
        lax.all_to_all(goal_keys, "goal", split_axis=2, concat_axis=0, tiled=True),
        lax.all_to_all(goal_values, "goal", split_axis=2, concat_axis=0, tiled=True),
    )
    query_heads = lax.all_to_all(queries, "goal", split_axis=2, concat_axis=0, tiled=True)
    attended = attend(query_heads, keys_heads, values_heads, goal_ids)
    merged = lax.all_to_all(attended, "goal", split_axis=0, concat_axis=2, tiled=True)
    live_rows = jnp.arange(merged.shape[1])[None, :] < tactic_len[:, None]
    context = jnp.where(live_rows[:, :, None], merged, jnp.zeros_like(merged))
    tact_local = context.shape[0]
    row_count = context.shape[1]
    flat = context.reshape(tact_local * row_count, context.shape[2])
    projected = jnp.dot(
        flat,
        lax.all_gather(out_weight, "goal", axis=0, tiled=True),
        preferred_element_type=jnp.float32,
    )
    return projected.astype(jnp.bfloat16).reshape(tact_local, row_count, out_weight.shape[1])


def attend_kernel(n, chunks, ids_ref, q_hbm, k_hbm, v_hbm, ctx_hbm,
                  ids_all, ids_smem, qb, ob,
                  send_sem, recv_sem, ids_send, ids_recv, local_sem, *held):
    keys_at, values_at = held[:chunks], held[chunks:]
    me = lax.axis_index("goal")
    tacts = q_hbm.shape[0]
    rows = q_hbm.shape[1]
    width = chunks * LANES

    def peer_of(i):
        return lax.rem(me + lax.rem(i * 7, n), n)

    def columns(owner, c):
        return pl.ds(pl.multiple_of(owner * width + c * LANES, LANES), LANES)

    def source(kind, c, owner):
        if kind == 0:
            return q_hbm.at[:, :, columns(owner, c)]
        return (k_hbm if kind == 1 else v_hbm).at[0, :, columns(owner, c)]

    def landing(kind, c, slot):
        if kind == 0:
            return qb.at[c, slot]
        return (keys_at if kind == 1 else values_at)[c].at[slot]

    def in_copy(kind, c, peer, slot_at_dest, recv_slot):
        return pltpu.make_async_remote_copy(
            src_ref=source(kind, c, peer),
            dst_ref=landing(kind, c, slot_at_dest),
            send_sem=send_sem.at[c * 4 + kind, peer],
            recv_sem=recv_sem.at[c * 4 + kind, recv_slot],
            device_id={"goal": peer},
            device_id_type=MESH,
        )

    def out_copy(c, peer, slot_at_dest, recv_slot):
        return pltpu.make_async_remote_copy(
            src_ref=ob.at[c, peer],
            dst_ref=ctx_hbm.at[:, :, columns(slot_at_dest, c)],
            send_sem=send_sem.at[c * 4 + 3, peer],
            recv_sem=recv_sem.at[c * 4 + 3, recv_slot],
            device_id={"goal": peer},
            device_id_type=MESH,
        )

    def ids_copy(peer, slot_at_dest, recv_slot):
        return pltpu.make_async_remote_copy(
            src_ref=ids_ref,
            dst_ref=ids_all.at[slot_at_dest],
            send_sem=ids_send.at[peer],
            recv_sem=ids_recv.at[recv_slot],
            device_id={"goal": peer},
            device_id_type=MESH,
        )

    def each_peer(body):
        def step(i, carry):
            body(peer_of(i))
            return carry
        lax.fori_loop(1, n, step, 0)

    barrier = pltpu.get_barrier_semaphore()
    each_peer(lambda p: pl.semaphore_signal(barrier, inc=1, device_id={"goal": p}, device_id_type=MESH))
    pl.semaphore_wait(barrier, n - 1)

    each_peer(lambda p: ids_copy(p, me, me).start())
    for c in range(chunks):
        for kind in (1, 0, 2):
            each_peer(lambda p, kind=kind, c=c: in_copy(kind, c, p, me, me).start())

    ids_all[me] = ids_ref[...]
    own = []
    for c in range(chunks):
        for kind in range(3):
            own.append(pltpu.make_async_copy(source(kind, c, me), landing(kind, c, me), local_sem.at[c * 4 + kind]))
    for copy in own:
        copy.start()
    for copy in own:
        copy.wait()

    each_peer(lambda p: ids_copy(p, p, p).wait_recv())
    to_scalar = pltpu.make_async_copy(ids_all, ids_smem, local_sem.at[3])
    to_scalar.start()
    to_scalar.wait()

    lane = lax.broadcasted_iota(jnp.int32, (rows, LANES), 1)
    first = lane < DH

    for c in range(chunks):
        for kind in (1, 0, 2):
            each_peer(lambda p, kind=kind, c=c: in_copy(kind, c, p, p, p).wait_recv())

        def one_tactic(p, t, c=c):
            goal = ids_smem[p, 0, t]
            q = qb[c, p, t]
            zero = jnp.zeros_like(q)
            both = jnp.concatenate([jnp.where(first, q, zero), jnp.where(first, zero, q)], axis=0)
            k = keys_at[c][goal]
            v = values_at[c][goal]
            s = lax.dot_general(both, k, (((1,), (1,)), ((), ())), preferred_element_type=jnp.float32)
            e = jnp.exp(s - jnp.max(s, axis=-1, keepdims=True))
            total = jnp.sum(e, axis=-1, keepdims=True)
            o = jnp.dot(e.astype(jnp.bfloat16), v, preferred_element_type=jnp.float32)
            o = o * (1.0 / total)
            ob[c, p, t] = jnp.where(first, o[:rows], o[rows:]).astype(jnp.bfloat16)

        def one_peer(p, c=c):
            for t in range(tacts):
                one_tactic(p, t)

        def step(i, carry, c=c):
            p = peer_of(i)
            one_peer(p)
            out_copy(c, p, me, me).start()
            return carry

        lax.fori_loop(1, n, step, 0)
        one_peer(me)
        back = pltpu.make_async_copy(ob.at[c, me], ctx_hbm.at[:, :, columns(me, c)], local_sem.at[c * 4 + 3])
        back.start()
        back.wait()

    each_peer(lambda p: ids_copy(p, me, me).wait_send())
    for c in range(chunks):
        for kind in range(3):
            each_peer(lambda p, kind=kind, c=c: in_copy(kind, c, p, me, me).wait_send())
    for c in range(chunks):
        each_peer(lambda p, c=c: out_copy(c, p, me, me).wait_send())
        each_peer(lambda p, c=c: out_copy(c, p, p, p).wait_recv())


def attend_exchange(n, ids, queries, goal_keys, goal_values):
    tacts, rows, features = queries.shape
    tokens = goal_keys.shape[1]
    chunks = features // n // LANES
    anywhere = pl.BlockSpec(memory_space=pl.ANY)
    bf16 = jnp.bfloat16
    return pl.pallas_call(
        functools.partial(attend_kernel, n, chunks),
        out_shape=jax.ShapeDtypeStruct(queries.shape, bf16),
        in_specs=[pl.BlockSpec(memory_space=pltpu.VMEM), anywhere, anywhere, anywhere],
        out_specs=anywhere,
        scratch_shapes=[
            pltpu.VMEM((n, 8, LANES), jnp.int32),
            pltpu.SMEM((n, 8, LANES), jnp.int32),
            pltpu.VMEM((chunks, n, tacts, rows, LANES), bf16),
            pltpu.VMEM((chunks, n, tacts, rows, LANES), bf16),
            pltpu.SemaphoreType.DMA((chunks * 4, n)),
            pltpu.SemaphoreType.DMA((chunks * 4, n)),
            pltpu.SemaphoreType.DMA((n,)),
            pltpu.SemaphoreType.DMA((n,)),
            pltpu.SemaphoreType.DMA((chunks * 4,)),
        ]
        + [pltpu.VMEM((n, tokens, LANES), bf16)] * (2 * chunks),
        compiler_params=pltpu.CompilerParams(
            collective_id=0, has_side_effects=True, vmem_limit_bytes=32 * 1024 * 1024
        ),
        cost_estimate=pl.CostEstimate(
            flops=8 * tacts * n * rows * tokens * features // n,
            bytes_accessed=400 * 1024 * 1024,
            transcendentals=0,
        ),
    )(ids, queries, goal_keys, goal_values)


def direct_shards(n, queries, goal_keys, goal_values, out_weight, tactic_goal, tactic_len):
    tacts, rows, features = queries.shape
    ids = jnp.pad(tactic_goal.reshape(1, tacts), ((0, 7), (0, LANES - tacts)))
    weight = lax.all_gather(out_weight, "goal", axis=0, tiled=True)
    context = attend_exchange(n, ids, queries, goal_keys, goal_values)
    projected = jnp.dot(
        context.reshape(tacts * rows, features), weight, preferred_element_type=jnp.float32
    ).astype(jnp.bfloat16).reshape(tacts, rows, weight.shape[1])
    live_rows = jnp.arange(rows)[None, :] < tactic_len[:, None]
    return jnp.where(live_rows[:, :, None], projected, jnp.zeros_like(projected))


def solution(mesh):
    n = mesh.shape["goal"]

    def shards(queries, goal_keys, goal_values, out_weight, tactic_goal, tactic_len):
        fits = (
            n > 1 and n % 7 != 0
            and queries.shape[2] % (n * LANES) == 0
            and goal_keys.shape[0] == 1
            and queries.shape[0] <= LANES
        )
        body = functools.partial(direct_shards, n) if fits else plain_shards
        return body(queries, goal_keys, goal_values, out_weight, tactic_goal, tactic_len)

    return jax.shard_map(
        shards,
        mesh=mesh,
        in_specs=(
            P(("groups", "goal"), None, None),
            P(("groups", "goal"), None, None),
            P(("groups", "goal"), None, None),
            P("goal", None),
            P(("groups", "goal"), None),
            P(("groups", "goal")),
        ),
        out_specs=P(("groups", "goal"), None, None),
        check_vma=False,
    )
```

time: 512 us -> 321 us (0.63)
  Pallas kernels: 0 us -> 288 us
  waiting for transfers between devices: 158 us -> 0.71 us
  local copies, waits for them, and re-layouts: 133 us -> 5.44 us
  other arithmetic: 70.9 us -> 1.18 us
  matrix products: 65.3 us -> 8.28 us
  blocking collectives: 44.1 us -> 0 us
  starting transfers between devices: 23.2 us -> 0.01 us
    pallas_call x0 -> x1, Pallas kernels: none -> 288 us  [attend_exchange(): pl.pallas_call(functools.partial(attend_kernel, n, chunks), out_shape=jax...]
    all_to_all x4 -> x0, waiting for transfers between devices: 157 us -> none  [the longest x1 58.2 us: shards(): lax.all_to_all(goal_values, 'goal', split_axis=2, concat_axis=0, tiled=True)]
    unnamed x22 -> x8, local copies, waits for them, and re-layouts: 75.4 us -> 4.78 us
    dot_general x3 -> x1, matrix products: 65.3 us -> 8.28 us  [direct_shards(): jnp.dot(context.reshape(tacts * rows, features), weight, preferred_elemen...]
    unnamed x2 -> x0, other arithmetic: 44.6 us -> none
    all_gather x1 -> x0, blocking collectives: 44.1 us -> none  [shards(): goal_ids = lax.all_gather(tactic_goal[:, 0], 'goal', axis=0, tiled=True)]
    select_n x2 -> x0, local copies, waits for them, and re-layouts: 23.8 us -> none  [the longest x1 11.9 us: attend_block(): jnp.take(keys_heads, block_ids, axis=0)]
    all_to_all x4 -> x0, starting transfers between devices: 23.2 us -> none  [the longest x1 7.53 us: shards(): lax.all_to_all(attended, 'goal', split_axis=0, concat_axis=2, tiled=True)]
  transfers between devices with their start and end apart: 5 -> 1, of which waited for: 3 -> 0; matrix products, arithmetic and copies ran while one was open for 51% -> 0% of each run, Pallas kernels for 0% -> 91%
where the time goes in v1:
time: 321 us; the launch traced here: 317 us
  Pallas kernels  288 us (90%)
  between operations  13.4 us (4%)
  matrix products  8.28 us (3%)
  local copies, waits for them, and re-layouts  5.44 us (2%)
    pallas_call x1, Pallas kernels, attend_exchange(): pl.pallas_call(functools.partial(attend_kernel, n, chunks), out_shape=jax...  288 us
    dot_general x1, matrix products, direct_shards(): jnp.dot(context.reshape(tacts * rows, features), weight, preferred_elemen...  8.28 us
  transfers between devices with their start and end apart: 1, of which 0 were waited for; matrix products, arithmetic and copies ran while one was open for 0% of the time, Pallas kernels for 91%

profile of v1, /device:TPU:13, one launch (start us, length us, event | category | flops | bytes accessed | tf_op | source)
XLA Modules:
  0.0 317.1 jit_solution(1880718715798649337)
XLA Ops:
  6.5 0.0 all-gather.2.cloned.1.call-start
  6.5 0.7 all-gather.2.cloned.1.call-update
  7.3 0.7 pad.4.ids_ref
  7.9 0.0 copy-start
  7.9 1.6 copy-done
  9.5 0.0 copy-start.1
  9.5 1.6 copy-done.1
  11.1 0.0 copy-start.2
  11.1 1.6 copy-done.2
  12.7 0.0 copy-start.3
  12.7 288.1 %shard_map.64 = bf16[4,64,4096]{2,1,0:T(8,128)(2,1)S(1)} custom-call(s32[8,128]{1,0:T(8,128)S(1)} %pad.4.ids_ref, bf16[4,64,4096]{2,1,0:T(8,128)(2,1)S(1)} %copy-done, bf16[1,256,4096]{2,1,0:T(8,128)(2,1)S(1)} %copy-done.1, bf16[1,256,4096]{2,1,0:T(8,128)(2,1)S(1)} %copy-done.2), custom_call_target="tpu_custom_call" | custom-call | flops 2147483648 | bytes 419430400 | tf_op jit(solution)/shard_map/pallas_call | solution.py:193
  300.8 0.0 copy-done.3
  300.8 0.1 iota_compare_fusion
  300.9 0.0 all-gather.2.cloned.1.call-done
  300.9 8.3 %convolution_convert_fusion = bf16[256,2048]{1,0:T(8,128)(2,1)S(1)} fusion(bf16[256,4096]{1,0:T(8,128)(2,1)S(1)} %bitcast.5, bf16[4096,2048]{1,0:T(8,128)(2,1)} %all-gather.2.cloned.1.call-done), kind=kOutput, calls=%fused_computation | convolution fusion | flops 4295491584 | bytes 19922944 | tf_op jit(solution)/shard_map/dot_general | solution.py:226
  309.2 1.1 broadcast_select_fusion
Async XLA Ops:
  6.5 294.4 %all-gather.2.cloned.1.call-start = ((), (), s32[]{:S(2)}) async-start(), calls=%async_computation | async-start | bytes 17825792 | tf_op jit(solution)/shard_map/all_gather | solution.py:224
  7.9 1.6 copy-start
  9.5 1.6 copy-start.1
  11.1 1.6 copy-start.2
  12.7 288.1 %copy-start.3 = (s32[4]{0:T(128)S(1)}, s32[4]{0:T(128)}, u32[]{:S(2)}) copy-start(s32[4]{0:T(128)} %param.11) | copy-start | bytes 52
Sparse Core Ops, SparseCore 0:
  9.5 241.9 all-gather.1

commit v2 on v1

--- a/solution.py
+++ b/solution.py
@@ -53,9 +53,9 @@
     return projected.astype(jnp.bfloat16).reshape(tact_local, row_count, out_weight.shape[1])
 
 
-def attend_kernel(n, chunks, ids_ref, q_hbm, k_hbm, v_hbm, ctx_hbm,
+def attend_kernel(n, chunks, ids_ref, q_hbm, k_hbm, v_hbm, w_hbm, ctx_hbm, w_all,
                   ids_all, ids_smem, qb, ob,
-                  send_sem, recv_sem, ids_send, ids_recv, local_sem, *held):
+                  send_sem, recv_sem, ids_send, ids_recv, local_sem, w_send, w_recv, w_local, *held):
     keys_at, values_at = held[:chunks], held[chunks:]
     me = lax.axis_index("goal")
     tacts = q_hbm.shape[0]
@@ -114,14 +114,114 @@
             return carry
         lax.fori_loop(1, n, step, 0)
 
+    group = lax.axis_index("groups")
+    half_rows = w_hbm.shape[0] // 2
+    z, y, core = me // 4, lax.rem(me // 2, 2), lax.rem(me, 2)
+    across = {"groups": 1 - group}
+    up, down = {"goal": lax.rem(me + 4, n)}, {"goal": lax.rem(me + n - 4, n)}
+    beside = {"goal": me + 2 - 4 * y}
+    twin = {"goal": me + 1 - 2 * core}
+
+    def half(ref, h):
+        return ref.at[pl.ds(pl.multiple_of(h * half_rows, half_rows), half_rows)]
+
+    def w_copy(slot, h, send, dest):
+        return pltpu.make_async_remote_copy(
+            src_ref=half(w_all.at[slot], h),
+            dst_ref=half(w_all.at[slot], h),
+            send_sem=w_send.at[send],
+            recv_sem=w_recv.at[slot * 2 + h],
+            device_id=dest,
+            device_id_type=MESH,
+        )
+
+    def own_copy(h, send, dest):
+        return pltpu.make_async_remote_copy(
+            src_ref=half(w_hbm, h),
+            dst_ref=half(w_all.at[me], h),
+            send_sem=w_send.at[send],
+            recv_sem=w_recv.at[me * 2 + h],
+            device_id=dest,
+            device_id_type=MESH,
+        )
+
+    def arrive(slot, h):
+        w_copy(slot, h, 0, twin).wait_recv()
+
+    w_own = pltpu.make_async_copy(w_hbm, w_all.at[me], w_local.at[0])
+    sends = []
+
+    def own_sends():
+        w_own.start()
+        for dest, send, when in ((up, 0, z < 3), (down, 1, z > 0)):
+            copy = own_copy(group, send, dest)
+            pl.when(when)(copy.start)
+            sends.append((copy, when))
+        copy = own_copy(group, 2, beside)
+        copy.start()
+        sends.append((copy, None))
+        for h in range(2):
+            copy = own_copy(h, 3 + h, twin)
+            copy.start()
+            sends.append((copy, None))
+
+    def z_steps():
+        for d in range(1, 4):
+            for side in range(2):
+                there = z - d if side == 0 else z + d
+                held_here = there >= 0 if side == 0 else there <= 3
+                slot = lax.rem(me + (n - 4 * d if side == 0 else 4 * d), n)
+                base = 5 + (d * 2 + side - 2) * 4
+                onward = held_here & (z < 3 if side == 0 else z > 0)
+                copies = [
+                    (w_copy(slot, group, base, up if side == 0 else down), onward),
+                    (w_copy(slot, group, base + 1, beside), held_here),
+                    (w_copy(slot, group, base + 2, across), held_here),
+                    (w_copy(slot, group, base + 3, twin), held_here),
+                ]
+                pl.when(held_here)(functools.partial(arrive, slot, group))
+                for copy, when in copies:
+                    pl.when(when)(copy.start)
+                    sends.append((copy, when))
+
+    def y_steps():
+        for d in range(4):
+            slot = lax.rem(me + 2 - 4 * y + 4 * d + n, n)
+            arrive(slot, group)
+            for copy in (w_copy(slot, group, 29 + 2 * d, across), w_copy(slot, group, 30 + 2 * d, twin)):
+                copy.start()
+                sends.append((copy, None))
+
+    def x_steps():
+        for d in range(1, 8):
+            slot = lax.rem(me + 2 * d, n)
+            arrive(slot, 1 - group)
+            copy = w_copy(slot, 1 - group, 36 + d, twin)
+            copy.start()
+            sends.append((copy, None))
+
+    def twin_steps():
+        for d in range(8):
+            for h in range(2):
+                arrive(lax.rem(me + 1 - 2 * core + 2 * d + n, n), h)
+        for copy, when in sends:
+            if when is None:
+                copy.wait_send()
+            else:
+                pl.when(when)(copy.wait_send)
+        w_own.wait()
+
     barrier = pltpu.get_barrier_semaphore()
+    pl.semaphore_signal(barrier, inc=1, device_id=across, device_id_type=MESH)
     each_peer(lambda p: pl.semaphore_signal(barrier, inc=1, device_id={"goal": p}, device_id_type=MESH))
-    pl.semaphore_wait(barrier, n - 1)
+    pl.semaphore_wait(barrier, n)
 
     each_peer(lambda p: ids_copy(p, me, me).start())
     for c in range(chunks):
         for kind in (1, 0, 2):
             each_peer(lambda p, kind=kind, c=c: in_copy(kind, c, p, me, me).start())
+        if c == 0:
+            own_sends()
 
     ids_all[me] = ids_ref[...]
     own = []
@@ -137,6 +237,9 @@
     to_scalar = pltpu.make_async_copy(ids_all, ids_smem, local_sem.at[3])
     to_scalar.start()
     to_scalar.wait()
+
+    z_steps()
+    y_steps()
 
     lane = lax.broadcasted_iota(jnp.int32, (rows, LANES), 1)
     first = lane < DH
@@ -174,7 +277,10 @@
         back = pltpu.make_async_copy(ob.at[c, me], ctx_hbm.at[:, :, columns(me, c)], local_sem.at[c * 4 + 3])
         back.start()
         back.wait()
-
+        if c == 0:
+            x_steps()
+
+    twin_steps()
     each_peer(lambda p: ids_copy(p, me, me).wait_send())
     for c in range(chunks):
         for kind in range(3):
@@ -184,7 +290,7 @@
         each_peer(lambda p, c=c: out_copy(c, p, p, p).wait_recv())
 
 
-def attend_exchange(n, ids, queries, goal_keys, goal_values):
+def attend_exchange(n, ids, queries, goal_keys, goal_values, out_weight):
     tacts, rows, features = queries.shape
     tokens = goal_keys.shape[1]
     chunks = features // n // LANES
@@ -192,9 +298,12 @@
     bf16 = jnp.bfloat16
     return pl.pallas_call(
         functools.partial(attend_kernel, n, chunks),
-        out_shape=jax.ShapeDtypeStruct(queries.shape, bf16),
-        in_specs=[pl.BlockSpec(memory_space=pltpu.VMEM), anywhere, anywhere, anywhere],
-        out_specs=anywhere,
+        out_shape=(
+            jax.ShapeDtypeStruct(queries.shape, bf16),
+            jax.ShapeDtypeStruct((n, *out_weight.shape), bf16),
+        ),
+        in_specs=[pl.BlockSpec(memory_space=pltpu.VMEM)] + [anywhere] * 4,
+        out_specs=(anywhere, anywhere),
         scratch_shapes=[
             pltpu.VMEM((n, 8, LANES), jnp.int32),
             pltpu.SMEM((n, 8, LANES), jnp.int32),
@@ -205,6 +314,9 @@
             pltpu.SemaphoreType.DMA((n,)),
             pltpu.SemaphoreType.DMA((n,)),
             pltpu.SemaphoreType.DMA((chunks * 4,)),
+            pltpu.SemaphoreType.DMA((44,)),
+            pltpu.SemaphoreType.DMA((2 * n,)),
+            pltpu.SemaphoreType.DMA((1,)),
         ]
         + [pltpu.VMEM((n, tokens, LANES), bf16)] * (2 * chunks),
         compiler_params=pltpu.CompilerParams(
@@ -215,14 +327,14 @@
             bytes_accessed=400 * 1024 * 1024,
             transcendentals=0,
         ),
-    )(ids, queries, goal_keys, goal_values)
+    )(ids, queries, goal_keys, goal_values, out_weight)
 
 
 def direct_shards(n, queries, goal_keys, goal_values, out_weight, tactic_goal, tactic_len):
     tacts, rows, features = queries.shape
     ids = jnp.pad(tactic_goal.reshape(1, tacts), ((0, 7), (0, LANES - tacts)))
-    weight = lax.all_gather(out_weight, "goal", axis=0, tiled=True)
-    context = attend_exchange(n, ids, queries, goal_keys, goal_values)
+    context, weight = attend_exchange(n, ids, queries, goal_keys, goal_values, out_weight)
+    weight = weight.reshape(features, out_weight.shape[1])
     projected = jnp.dot(
         context.reshape(tacts * rows, features), weight, preferred_element_type=jnp.float32
     ).astype(jnp.bfloat16).reshape(tacts, rows, weight.shape[1])
@@ -235,7 +347,8 @@
 
     def shards(queries, goal_keys, goal_values, out_weight, tactic_goal, tactic_len):
         fits = (
-            n > 1 and n % 7 != 0
+            n == 16 and mesh.shape["groups"] == 2
+            and out_weight.shape[0] % 32 == 0
             and queries.shape[2] % (n * LANES) == 0
             and goal_keys.shape[0] == 1
             and queries.shape[0] <= LANES

time: 321 us -> 277 us (0.86)
  Pallas kernels: 288 us -> 258 us
  between operations: 13.4 us -> 0.04 us
    pallas_call x1, Pallas kernels: 288 us -> 258 us  [attend_exchange(): pl.pallas_call(functools.partial(attend_kernel, n, chunks), out_shape=(ja...]
  transfers between devices with their start and end apart: 1 -> 0, of which waited for: 0 -> 0; matrix products, arithmetic and copies ran while one was open for 0% -> 0% of each run, Pallas kernels for 91% -> 0%
where the time goes in v2:
time: 277 us; the launch traced here: 274 us
  Pallas kernels  258 us (93%)
  matrix products  8.29 us (3%)
  local copies, waits for them, and re-layouts  6.66 us (2%)
    pallas_call x1, Pallas kernels, attend_exchange(): pl.pallas_call(functools.partial(attend_kernel, n, chunks), out_shape=(ja...  258 us
    dot_general x1, matrix products, direct_shards(): jnp.dot(context.reshape(tacts * rows, features), weight, preferred_elemen...  8.29 us
    unnamed x10, local copies, waits for them, and re-layouts  6 us

profile of v2, /device:TPU:13, one launch (start us, length us, event | category | flops | bytes accessed | tf_op | source)
XLA Modules:
  0.0 274.0 jit_solution(5887890344344793118)
XLA Ops:
  0.0 0.7 pad.4.ids_ref
  0.7 0.0 copy-start
  0.7 1.6 copy-done
  2.3 0.0 copy-start.1
  2.3 1.6 copy-done.1
  3.8 0.0 copy-start.2
  3.8 1.6 copy-done.2
  5.4 0.0 copy-start.3
  5.4 1.2 copy-done.3
  6.7 257.9 %shard_map.64 = (bf16[4,64,4096]{2,1,0:T(8,128)(2,1)S(1)}, bf16[16,256,2048]{2,1,0:T(8,128)(2,1)}) custom-call(s32[8,128]{1,0:T(8,128)S(1)} %pad.4.ids_ref, bf16[4,64,4096]{2,1,0:T(8,128)(2,1)S(1)} %copy-done, bf16[1,256,4096]{2,1,0:T(8,128)(2,1)S(1)} %copy-done.1, bf16[1,256,4096]{2,1,0:T(8,128)(2,1)S(1)} %copy-done.2, bf16[256,2048]{1,0:T(8,128)(2,1)S(1)} %copy-done.3), custom_call_target="tpu_custom_call" | custom-call | flops 2147483648 | bytes 419430400 | tf_op jit(solution)/shard_map/pallas_call | solution.py:299
  264.5 0.0 copy-start.4
  264.5 8.3 %convolution_convert_fusion = bf16[256,2048]{1,0:T(8,128)(2,1)S(1)} fusion(bf16[256,4096]{1,0:T(8,128)(2,1)S(1)} %bitcast.6, bf16[4096,2048]{1,0:T(8,128)(2,1)} %bitcast.9), kind=kOutput, calls=%fused_computation | convolution fusion | flops 4295491584 | bytes 19922944 | tf_op jit(solution)/shard_map/dot_general | solution.py:338
  272.8 0.0 copy-done.4
  272.9 0.1 iota_compare_fusion
  272.9 1.1 broadcast_select_fusion
Async XLA Ops:
  0.7 1.6 copy-start
  2.3 1.6 copy-start.1
  3.8 1.6 copy-start.2
  5.4 1.2 copy-start.3
  264.5 8.3 %copy-start.4 = (s32[4]{0:T(128)S(1)}, s32[4]{0:T(128)}, u32[]{:S(2)}) copy-start(s32[4]{0:T(128)} %param.11) | copy-start | bytes 52

commit v3 on v2

--- a/solution.py
+++ b/solution.py
@@ -165,8 +165,8 @@
             copy.start()
             sends.append((copy, None))
 
-    def z_steps():
-        for d in range(1, 4):
+    def z_steps(distances):
+        for d in distances:
             for side in range(2):
                 there = z - d if side == 0 else z + d
                 held_here = there >= 0 if side == 0 else there <= 3
@@ -216,12 +216,16 @@
     each_peer(lambda p: pl.semaphore_signal(barrier, inc=1, device_id={"goal": p}, device_id_type=MESH))
     pl.semaphore_wait(barrier, n)
 
+    batches = [(c, kind) for c in range(chunks) for kind in (1, 0, 2)]
+
+    def issue(count):
+        for _ in range(min(count, len(batches))):
+            c, kind = batches.pop(0)
+            each_peer(lambda p: in_copy(kind, c, p, me, me).start())
+
+    own_sends()
     each_peer(lambda p: ids_copy(p, me, me).start())
-    for c in range(chunks):
-        for kind in (1, 0, 2):
-            each_peer(lambda p, kind=kind, c=c: in_copy(kind, c, p, me, me).start())
-        if c == 0:
-            own_sends()
+    issue(2)
 
     ids_all[me] = ids_ref[...]
     own = []
@@ -238,8 +242,14 @@
     to_scalar.start()
     to_scalar.wait()
 
-    z_steps()
+    z_steps((1,))
+    issue(1)
+    z_steps((2,))
+    issue(1)
+    z_steps((3,))
+    issue(1)
     y_steps()
+    issue(len(batches))
 
     lane = lax.broadcasted_iota(jnp.int32, (rows, LANES), 1)
     first = lane < DH
@@ -320,7 +330,7 @@
         ]
         + [pltpu.VMEM((n, tokens, LANES), bf16)] * (2 * chunks),
         compiler_params=pltpu.CompilerParams(
-            collective_id=0, has_side_effects=True, vmem_limit_bytes=32 * 1024 * 1024
+            collective_id=0, has_side_effects=True, vmem_limit_bytes=60 * 1024 * 1024
         ),
         cost_estimate=pl.CostEstimate(
             flops=8 * tacts * n * rows * tokens * features // n,

time: 277 us -> 229 us (0.83)
  Pallas kernels: 258 us -> 212 us
  local copies, waits for them, and re-layouts: 6.66 us -> 1.26 us
    pallas_call x1, Pallas kernels: 258 us -> 212 us  [attend_exchange(): pl.pallas_call(functools.partial(attend_kernel, n, chunks), out_shape=(ja...]
    unnamed x10 -> x2, local copies, waits for them, and re-layouts: 6 us -> 0.01 us
where the time goes in v3:
time: 229 us; the launch traced here: 225 us
  Pallas kernels  212 us (93%)
  matrix products  10.9 us (5%)
    pallas_call x1, Pallas kernels, attend_exchange(): pl.pallas_call(functools.partial(attend_kernel, n, chunks), out_shape=(ja...  212 us
    dot_general x1, matrix products, direct_shards(): jnp.dot(context.reshape(tacts * rows, features), weight, preferred_elemen...  10.9 us

profile of v3, /device:TPU:13, one launch (start us, length us, event | category | flops | bytes accessed | tf_op | source)
XLA Modules:
  0.0 224.9 jit_solution(12667054293254504471)
XLA Ops:
  0.0 1.3 pad.4.ids_ref
  1.3 211.5 %shard_map.64 = (bf16[4,64,4096]{2,1,0:T(8,128)(2,1)}, bf16[16,256,2048]{2,1,0:T(8,128)(2,1)}) custom-call(s32[8,128]{1,0:T(8,128)} %pad.4.ids_ref, bf16[4,64,4096]{2,1,0:T(8,128)(2,1)} %q_hbm.1, bf16[1,256,4096]{2,1,0:T(8,128)(2,1)} %k_hbm.1, bf16[1,256,4096]{2,1,0:T(8,128)(2,1)} %v_hbm.1, bf16[256,2048]{1,0:T(8,128)(2,1)} %w_hbm.1), custom_call_target="tpu_custom_call" | custom-call | flops 2147483648 | bytes 419430400 | tf_op jit(solution)/shard_map/pallas_call | solution.py:309
  212.8 0.0 copy-start
  212.8 10.9 %convolution_convert_fusion = bf16[256,2048]{1,0:T(8,128)(2,1)S(1)} fusion(bf16[256,4096]{1,0:T(8,128)(2,1)} %bitcast.9, bf16[4096,2048]{1,0:T(8,128)(2,1)} %bitcast.8), kind=kOutput, calls=%fused_computation | convolution fusion | flops 4295491584 | bytes 19922944 | tf_op jit(solution)/shard_map/dot_general | solution.py:348
  223.7 0.0 copy-done
  223.7 0.1 iota_compare_fusion
  223.8 1.1 broadcast_select_fusion
Async XLA Ops:
  212.8 10.9 %copy-start = (s32[4]{0:T(128)S(1)}, s32[4]{0:T(128)}, u32[]{:S(2)}) copy-start(s32[4]{0:T(128)} %param.11) | copy-start | bytes 52

commit v4 on v3

--- a/solution.py
+++ b/solution.py
@@ -63,7 +63,7 @@
     width = chunks * LANES
 
     def peer_of(i):
-        return lax.rem(me + lax.rem(i * 7, n), n)
+        return lax.rem(me + i, n)
 
     def columns(owner, c):
         return pl.ds(pl.multiple_of(owner * width + c * LANES, LANES), LANES)
@@ -234,14 +234,6 @@
             own.append(pltpu.make_async_copy(source(kind, c, me), landing(kind, c, me), local_sem.at[c * 4 + kind]))
     for copy in own:
         copy.start()
-    for copy in own:
-        copy.wait()
-
-    each_peer(lambda p: ids_copy(p, p, p).wait_recv())
-    to_scalar = pltpu.make_async_copy(ids_all, ids_smem, local_sem.at[3])
-    to_scalar.start()
-    to_scalar.wait()
-
     z_steps((1,))
     issue(1)
     z_steps((2,))
@@ -250,6 +242,14 @@
     issue(1)
     y_steps()
     issue(len(batches))
+
+    for copy in own:
+        copy.wait()
+
+    each_peer(lambda p: ids_copy(p, p, p).wait_recv())
+    to_scalar = pltpu.make_async_copy(ids_all, ids_smem, local_sem.at[3])
+    to_scalar.start()
+    to_scalar.wait()
 
     lane = lax.broadcasted_iota(jnp.int32, (rows, LANES), 1)
     first = lane < DH
@@ -347,9 +347,10 @@
     weight = weight.reshape(features, out_weight.shape[1])
     projected = jnp.dot(
         context.reshape(tacts * rows, features), weight, preferred_element_type=jnp.float32
-    ).astype(jnp.bfloat16).reshape(tacts, rows, weight.shape[1])
-    live_rows = jnp.arange(rows)[None, :] < tactic_len[:, None]
-    return jnp.where(live_rows[:, :, None], projected, jnp.zeros_like(projected))
+    )
+    live_rows = (jnp.arange(rows)[None, :] < tactic_len[:, None]).reshape(tacts * rows, 1)
+    projected = jnp.where(live_rows, projected, 0.0).astype(jnp.bfloat16)
+    return projected.reshape(tacts, rows, weight.shape[1])
 
 
 def solution(mesh):

time: 229 us -> 228 us (level); the launches traced: 225 us -> 228 us
  no operation moved by 1% of the time
where the time goes in v4:
time: 228 us
  Pallas kernels  214 us (94%)
  matrix products  11.9 us (5%)
    pallas_call x1, Pallas kernels, attend_exchange(): pl.pallas_call(functools.partial(attend_kernel, n, chunks), out_shape=(ja...  214 us
    dot_general x1, matrix products, direct_shards(): jnp.dot(context.reshape(tacts * rows, features), weight, preferred_elemen...  11.9 us

profile of v4, /device:TPU:13, one launch (start us, length us, event | category | flops | bytes accessed | tf_op | source)
XLA Modules:
  0.0 227.6 jit_solution(7908028467329359597)
XLA Ops:
  0.0 0.7 iota_compare_fusion
  0.7 0.1 lt.23
  0.8 1.3 pad.4.ids_ref
  2.1 213.7 %shard_map.64 = (bf16[4,64,4096]{2,1,0:T(8,128)(2,1)}, bf16[16,256,2048]{2,1,0:T(8,128)(2,1)}) custom-call(s32[8,128]{1,0:T(8,128)} %pad.4.ids_ref, bf16[4,64,4096]{2,1,0:T(8,128)(2,1)} %q_hbm.1, bf16[1,256,4096]{2,1,0:T(8,128)(2,1)} %k_hbm.1, bf16[1,256,4096]{2,1,0:T(8,128)(2,1)} %v_hbm.1, bf16[256,2048]{1,0:T(8,128)(2,1)} %w_hbm.1), custom_call_target="tpu_custom_call" | custom-call | flops 2147483648 | bytes 419430400 | tf_op jit(solution)/shard_map/pallas_call | solution.py:309
  215.7 11.9 %fusion = bf16[256,2048]{1,0:T(8,128)(2,1)} fusion(bf16[256,4096]{1,0:T(8,128)(2,1)} %bitcast.8, bf16[4096,2048]{1,0:T(8,128)(2,1)} %bitcast.7, pred[256]{0:T(512)(128)(4,1)S(1)} %lt.23), kind=kOutput, calls=%fused_computation.1 | convolution fusion | flops 4296015872 | bytes 19923200 | tf_op jit(solution)/shard_map/dot_general | solution.py:348
